TPU v7x, 128 devices: a whole 4x4x4 slice. The times are simulated.
128 devices in a mesh: blk: 16 (over x, y_lo, core), grp: 8 (over z, y_hi).
Axes of the slice: x: 4, y: 4 (y_hi: 2, y_lo: 2; y = y_hi * 2 + y_lo), z: 4, core: 2. Of those that a mesh axis runs over, the one named last changes fastest.
Arguments:
- hidden: bfloat16 [131072, 2048], P(('blk', 'grp')), may hold values from -24 to 24
- weight: bfloat16 [2048, 512], replicated, may hold values from -0.125 to 0.125
- stamps: int32 [131072], P(('blk', 'grp')), may hold values from 0 to 511
- group_ids: int32 [131072], P(('blk', 'grp')), may hold values from 0 to 255
Outputs:
- grad_hidden: bfloat16 [131072, 2048], P(('blk', 'grp'))
- grad_weight: float32 [2048, 512], P(('blk', 'grp'))
- loss: float32 [], replicated
All inputs are finite; a program needn't handle non-finite values.
Results may differ from a plain program's by a relative error of at most 0.0065.
Values may be sent and summed in bfloat16 or wider, within the bound.
A program may use at most 64 MiB of HBM per device.

v0:
```python
import math

import jax
import jax.numpy as jnp
from jax import lax
from jax.sharding import PartitionSpec as P

D = 512
TAU = 64


def swapped(value, axis, apart):
    return lax.ppermute(value, axis, [(i, i ^ 1 << apart) for i in range(lax.axis_size(axis))])


def pair_terms(left_emb, left_stamp, left_ids, right_emb, right_stamp, right_ids, keep_mask):
    inv_root = 1.0 / math.sqrt(D)
    scores = (
        jnp.einsum("...id,...jd->...ij", left_emb, right_emb, preferred_element_type=jnp.float32)
        * inv_root
    )
    gap_size = jnp.abs(left_stamp[..., :, None] - right_stamp[..., None, :]).astype(jnp.float32)
    pair_weights = jnp.exp(-gap_size / TAU) * keep_mask
    label_sign = jnp.where(left_ids[..., :, None] == right_ids[..., None, :], 1.0, -1.0).astype(
        jnp.float32
    )
    margin = -label_sign * scores
    losses = pair_weights * jax.nn.softplus(margin)
    coefficient = (pair_weights * -label_sign * jax.nn.sigmoid(margin) * inv_root).astype(
        jnp.bfloat16
    )
    return (coefficient, pair_weights, losses)


def trade_rows(embedded, stamps, group_ids, along_blk, bit_number):
    if along_blk:
        return swapped((embedded, stamps, group_ids), "blk", bit_number)
    return swapped((embedded, stamps, group_ids), "grp", bit_number)


def trade_grads(partner_grad, along_blk, bit_number):
    if along_blk:
        return swapped(partner_grad, "blk", bit_number)
    return swapped(partner_grad, "grp", bit_number)


def side_of(along_blk, bit_number):
    place = lax.axis_index("blk") if along_blk else lax.axis_index("grp")
    return place // 2**bit_number % 2


def turned(values, own_side, half_rows):
    return jnp.where(own_side == 1, jnp.roll(values, half_rows, 0), values)


def on_device(hidden, weight, stamps, group_ids):
    row_count = hidden.shape[0]
    half_rows = row_count // 2
    emb_width = weight.shape[1]
    device_count = lax.axis_size("blk") * lax.axis_size("grp")
    embedded = jnp.dot(hidden, weight, preferred_element_type=jnp.float32).astype(jnp.bfloat16)
    row_index = lax.iota(jnp.int32, row_count)
    offdiag = (row_index[:, None] != row_index[None, :]).astype(jnp.float32)
    coefficient, pair_weights, losses = pair_terms(
        embedded, stamps, group_ids, embedded, stamps, group_ids, offdiag
    )
    accum = jnp.dot(coefficient, embedded, preferred_element_type=jnp.float32)
    weight_sum = 0.5 * jnp.sum(pair_weights)
    loss_sum = 0.5 * jnp.sum(losses)
    round_plan = [
        (True, 0),
        (False, lax.axis_size("grp").bit_length() - 2),
        (True, lax.axis_size("blk").bit_length() - 2),
    ]
    for along_blk, bit_number in round_plan:
        other_emb, other_stamp, other_ids = trade_rows(
            embedded, stamps, group_ids, along_blk, bit_number
        )
        own_side = side_of(along_blk, bit_number)
        their_emb = turned(other_emb, own_side, half_rows).reshape(2, half_rows, emb_width)
        their_stamp = turned(other_stamp, own_side, half_rows).reshape(2, half_rows)
        their_ids = turned(other_ids, own_side, half_rows).reshape(2, half_rows)
        mine_emb = embedded.reshape(2, half_rows, emb_width)
        coefficient, pair_weights, losses = pair_terms(
            mine_emb,
            stamps.reshape(2, half_rows),
            group_ids.reshape(2, half_rows),
            their_emb,
            their_stamp,
            their_ids,
            1.0,
        )
        accum = accum + jnp.einsum(
            "qij,qjd->qid", coefficient, their_emb, preferred_element_type=jnp.float32
        ).reshape(row_count, emb_width)
        back_grad = jnp.einsum(
            "qij,qid->qjd", coefficient, mine_emb, preferred_element_type=jnp.float32
        ).reshape(row_count, emb_width)
        accum = accum + trade_grads(turned(back_grad, own_side, half_rows), along_blk, bit_number)
        weight_sum = weight_sum + jnp.sum(pair_weights)
        loss_sum = loss_sum + jnp.sum(losses)
    summed = accum.astype(jnp.bfloat16)
    pair_count = (
        device_count * row_count * (row_count - 1) // 2
        + 3 * device_count * row_count * row_count // 2
    )
    weight_total, pair_loss = lax.psum((weight_sum, loss_sum), ("blk", "grp"))
    partial_grad = lax.psum_scatter(
        lax.dot_general(
            hidden, summed, (((0,), (0,)), ((), ())), preferred_element_type=jnp.float32
        ),
        ("blk", "grp"),
        scatter_dimension=0,
        tiled=True,
    )
    mean_weight = weight_total / float(pair_count)
    grad_hidden = (
        lax.dot_general(
            summed, weight, (((1,), (1,)), ((), ())), preferred_element_type=jnp.float32
        )
        / mean_weight
    ).astype(jnp.bfloat16)
    grad_weight = partial_grad / (mean_weight * float(device_count * row_count))
    loss = pair_loss / weight_total
    return (grad_hidden, grad_weight, loss)


def solution(mesh):
    in_specs = (P(("blk", "grp"), None), P(), P(("blk", "grp")), P(("blk", "grp")))
    out_specs = (P(("blk", "grp"), None), P(("blk", "grp"), None), P())
    return jax.shard_map(
        on_device, mesh=mesh, in_specs=in_specs, out_specs=out_specs, check_vma=False
    )
```

profile of v0, /device:TPU:0, one launch (start us, length us, event | category | flops | bytes accessed | tf_op | source)
XLA Modules:
  0.0 795.6 jit_solution(14211856900151437855)
XLA Ops:
  7.2 0.0 reduce-scatter.4.cloned.1.call-start
  7.2 0.1 collective-permute-start
  7.3 3.2 collective-permute-start.8
  10.5 3.9 collective-permute-start.4
  14.4 0.5 collective-permute-start.9
  14.9 4.5 convolution_convert_fusion
  19.6 0.2 collective-permute-start.5
  19.8 3.0 collective-permute-start.10
  22.9 3.4 collective-permute-start.6
  26.5 23.0 %collective-permute-done.6 = bf16[1024,512]{1,0:T(8,128)(2,1)} collective-permute-done((bf16[1024,512]{1,0:T(8,128)(2,1)S(1)}, bf16[1024,512]{1,0:T(8,128)(2,1)}, u32[]{:S(2)}, u32[]{:S(2)}) %collective-permute-start.6) | collective-permute-done | bytes 1048608 | tf_op jit(solution)/shard_map/ppermute | solution.py:13
  49.4 1.3 fusion.20
  50.7 1.5 maximum_select_fusion.4
  52.2 1.3 fusion.19
  53.5 1.5 maximum_select_fusion.3
  55.1 1.4 fusion.11
  56.5 1.4 fusion.12
  58.0 1.3 fusion.21
  59.2 1.5 maximum_select_fusion.5
  60.8 1.4 fusion.13
  62.2 9.0 %multiply_reduce_fusion = (f32[]{:T(128)}, f32[]{:T(128)}, f32[]{:T(128)}, f32[]{:T(128)}, f32[]{:T(128)}, /*index=5*/f32[]{:T(128)}, bf16[2,512,512]{2,1,0:T(8,...) fusion(f32[2,512,512]{2,1,0:T(8,128)S(1)} %get-tuple-element.52, s32[2,512]{1,0:T(2,128)S(1)} %sub.77, ...), kind=kLoop, calls=%fused_computation.28 | loop fusion | flops 41418748 | bytes 10256408 | tf_op jit(solution)/shard_map/reduce_sum | solution.py:101
  71.2 0.8 fusion.29
  72.0 0.8 fusion.31
  72.7 0.8 fusion.33
  73.5 0.2 slice_bitcast_fusion.1
  73.7 0.2 slice_bitcast_fusion.3
  73.9 0.2 slice_bitcast_fusion.5
  74.0 0.5 maximum_select_fusion
  74.6 0.1 collective-permute-start.3
  74.6 0.5 maximum_select_fusion.1
  75.2 2.0 collective-permute-start.7
  77.2 0.5 maximum_select_fusion.2
  77.7 0.3 collective-permute-start.11
  78.0 5.5 fusion.1
  83.5 0.7 fusion.28
  84.2 0.7 fusion.30
  84.9 0.7 fusion.32
  85.6 39.1 %collective-permute-done.7 = f32[1024,512]{1,0:T(8,128)S(1)} collective-permute-done((f32[1024,512]{1,0:T(8,128)S(1)}, f32[1024,512]{1,0:T(8,128)S(1)}, u32[]{:S(2)}, u32[]{:S(2)}) %collective-permute-start.7) | collective-permute-done | bytes 2097184 | tf_op jit(solution)/shard_map/ppermute | solution.py:13
  124.8 2.5 collective-permute-done.11
  127.2 5.3 fusion.4
  132.5 1.0 copy-done.2
  133.5 4.5 convolution_bitcast_fusion
  137.9 5.4 copy.18
  143.3 0.0 reduce-scatter.4.cloned.1.call-update
  148.3 65.2 %all-reduce = (f32[]{:T(128)}, f32[]{:T(128)}) all-reduce(f32[]{:T(128)S(6)} %add.96, f32[]{:T(128)S(6)} %add.103), channel_id=1, replica_groups=mesh['blk'=16,'grp'=8] {'blk','grp'}, use_global_device_ids=true, to_apply=%region_4.5 | all-reduce | flops 2 | bytes 16 | tf_op jit(solution)/shard_map/psum | solution.py:107
  216.2 4.4 divide_convert_fusion
  220.6 565.4 %reduce-scatter.4.cloned.1.call-done = f32[16,512]{1,0:T(8,128)} async-done(((f32[2048,512]{1,0:T(8,128)}), f32[16,512]{1,0:T(8,128)}) %reduce-scatter.4.cloned.1.call-update) | async-done | bytes 32784
  786.0 0.9 copy.19
  786.9 0.7 copy.14
  (43 shorter events, 0.2 us)
Async XLA Ops:
  7.2 7.8 copy-start
  7.2 12.3 %copy-start.5 = (s32[1024]{0:T(1024)S(1)}, s32[1024]{0:T(1024)}, u32[]{:S(2)}) copy-start(s32[1024]{0:T(1024)} %param.6) | copy-start | bytes 12292
  7.2 12.3 %copy-start.4 = (s32[1024]{0:T(1024)S(1)}, s32[1024]{0:T(1024)}, u32[]{:S(2)}) copy-start(s32[1024]{0:T(1024)} %param.7) | copy-start | bytes 12292
  7.2 778.8 %reduce-scatter.4.cloned.1.call-start = ((), (), s32[]{:S(2)}) async-start(), calls=%async_computation.1 | async-start | bytes 4227072
  7.2 12.3 %collective-permute-start = (s32[1024]{0:T(1024)}, s32[1024]{0:T(1024)S(1)}, u32[]{:S(2)}, u32[]{:S(2)}) collective-permute-start(s32[1024]{0:T(1024)} %param.6), channel_id=1, source_target_pairs={{0,8},{8,0},{16,24},{24,16},{32,40},{40,32},{48,56},{56,48},{64,72... | collective-permute-start | bytes 12296 | tf_op jit(solution)/shard_map/ppermute | solution.py:13
  7.3 12.5 %collective-permute-start.8 = (s32[1024]{0:T(1024)}, s32[1024]{0:T(1024)S(1)}, u32[]{:S(2)}, u32[]{:S(2)}) collective-permute-start(s32[1024]{0:T(1024)} %param.6), channel_id=1, source_target_pairs={{0,64},{8,72},{16,80},{24,88},{32,96},{40,104},{48,112},{56,120},{... | collective-permute-start | bytes 12296 | tf_op jit(solution)/shard_map/ppermute | solution.py:13
  10.5 12.3 %collective-permute-start.4 = (s32[1024]{0:T(1024)}, s32[1024]{0:T(1024)S(1)}, u32[]{:S(2)}, u32[]{:S(2)}) collective-permute-start(s32[1024]{0:T(1024)} %param.6), channel_id=1, source_target_pairs={{0,4},{1,5},{2,6},{3,7},{4,0},{5,1},{6,2},{7,3},{8,12},{9,13},{10,... | collective-permute-start | bytes 12296 | tf_op jit(solution)/shard_map/ppermute | solution.py:13
  14.4 11.8 %collective-permute-start.1 = (s32[1024]{0:T(1024)}, s32[1024]{0:T(1024)S(1)}, u32[]{:S(2)}, u32[]{:S(2)}) collective-permute-start(s32[1024]{0:T(1024)} %param.7), channel_id=1, source_target_pairs={{0,8},{8,0},{16,24},{24,16},{32,40},{40,32},{48,56},{56,48},{64,72... | collective-permute-start | bytes 12296 | tf_op jit(solution)/shard_map/ppermute | solution.py:13
  14.4 11.8 %collective-permute-start.9 = (s32[1024]{0:T(1024)}, s32[1024]{0:T(1024)S(1)}, u32[]{:S(2)}, u32[]{:S(2)}) collective-permute-start(s32[1024]{0:T(1024)} %param.7), channel_id=1, source_target_pairs={{0,64},{8,72},{16,80},{24,88},{32,96},{40,104},{48,112},{56,120},{... | collective-permute-start | bytes 12296 | tf_op jit(solution)/shard_map/ppermute | solution.py:13
  19.6 6.8 collective-permute-start.5
  19.8 38.1 %collective-permute-start.10 = (bf16[1024,512]{1,0:T(8,128)(2,1)S(1)}, bf16[1024,512]{1,0:T(8,128)(2,1)}, u32[]{:S(2)}, u32[]{:S(2)}) collective-permute-start(bf16[1024,512]{1,0:T(8,128)(2,1)S(1)} %convolution_convert_fusion), channel_id=1, source_target_pairs={{0,64},{8,72},{16,80},{24,88},{32,96},{40,104},{48,112},{56,120},{... | collective-permute-start | bytes 3145736 | tf_op jit(solution)/shard_map/ppermute | solution.py:13
  22.9 26.6 %collective-permute-start.6 = (bf16[1024,512]{1,0:T(8,128)(2,1)S(1)}, bf16[1024,512]{1,0:T(8,128)(2,1)}, u32[]{:S(2)}, u32[]{:S(2)}) collective-permute-start(bf16[1024,512]{1,0:T(8,128)(2,1)S(1)} %convolution_convert_fusion), channel_id=1, source_target_pairs={{0,4},{1,5},{2,6},{3,7},{4,0},{5,1},{6,2},{7,3},{8,12},{9,13},{10,... | collective-permute-start | bytes 3145736 | tf_op jit(solution)/shard_map/ppermute | solution.py:13
  26.2 26.0 %collective-permute-start.2 = (bf16[1024,512]{1,0:T(8,128)(2,1)S(1)}, bf16[1024,512]{1,0:T(8,128)(2,1)}, u32[]{:S(2)}, u32[]{:S(2)}) collective-permute-start(bf16[1024,512]{1,0:T(8,128)(2,1)S(1)} %convolution_convert_fusion), channel_id=1, source_target_pairs={{0,8},{8,0},{16,24},{24,16},{32,40},{40,32},{48,56},{56,48},{64,72... | collective-permute-start | bytes 3145736 | tf_op jit(solution)/shard_map/ppermute | solution.py:13
  74.6 11.1 %collective-permute-start.3 = (f32[1024,512]{1,0:T(8,128)S(1)}, f32[1024,512]{1,0:T(8,128)S(1)}, u32[]{:S(2)}, u32[]{:S(2)}) collective-permute-start(f32[1024,512]{1,0:T(8,128)S(1)} %maximum_select_fusion), channel_id=1, source_target_pairs={{0,8},{8,0},{16,24},{24,16},{32,40},{40,32},{48,56},{56,48},{64,72... | collective-permute-start | bytes 6291464 | tf_op jit(solution)/shard_map/ppermute | solution.py:13
  75.2 49.6 %collective-permute-start.7 = (f32[1024,512]{1,0:T(8,128)S(1)}, f32[1024,512]{1,0:T(8,128)S(1)}, u32[]{:S(2)}, u32[]{:S(2)}) collective-permute-start(f32[1024,512]{1,0:T(8,128)S(1)} %maximum_select_fusion.1), channel_id=1, source_target_pairs={{0,4},{1,5},{2,6},{3,7},{4,0},{5,1},{6,2},{7,3},{8,12},{9,13},{10,... | collective-permute-start | bytes 6291464 | tf_op jit(solution)/shard_map/ppermute | solution.py:13
  77.7 49.6 %collective-permute-start.11 = (f32[1024,512]{1,0:T(8,128)S(1)}, f32[1024,512]{1,0:T(8,128)S(1)}, u32[]{:S(2)}, u32[]{:S(2)}) collective-permute-start(f32[1024,512]{1,0:T(8,128)S(1)} %maximum_select_fusion.2), channel_id=1, source_target_pairs={{0,64},{8,72},{16,80},{24,88},{32,96},{40,104},{48,112},{56,120},{... | collective-permute-start | bytes 6291464 | tf_op jit(solution)/shard_map/ppermute | solution.py:13
  127.2 6.3 copy-start.1
  132.5 1.0 copy-start.2
  143.3 72.9 %copy-start.3 = (bf16[1024,512]{1,0:T(8,128)(2,1)S(1)}, bf16[1024,512]{1,0:T(8,128)(2,1)}, u32[]{:S(2)}) copy-start(bf16[1024,512]{1,0:T(8,128)(2,1)} %copy-done.2) | copy-start | bytes 3145732
Sparse Core Ops, SparseCore 0:
  143.4 642.5 reduce-scatter.3
where the time goes:
time: 796 us
  waiting for transfers between devices  630 us (79%)
  blocking collectives  65.2 us (8%)
  matrix products  32.8 us (4%)
  between operations  23.3 us (3%)
  starting transfers between devices  16.7 us (2%)
  other arithmetic  15.2 us (2%)
  local copies, waits for them, and re-layouts  12.4 us (2%)
    unnamed x2, waiting for transfers between devices  565 us
    psum x1, blocking collectives, on_device(): weight_total, pair_loss = lax.psum((weight_sum, loss_sum), ('blk', 'grp'))  65.2 us
    ppermute x12, waiting for transfers between devices, swapped(): lax.ppermute(value, axis, [(i, i ^ 1 << apart) for i in range(lax.axis_si...  64.6 us
    ppermute x12, starting transfers between devices, swapped(): lax.ppermute(value, axis, [(i, i ^ 1 << apart) for i in range(lax.axis_si...  16.7 us
  transfers between devices with their start and end apart: 13, of which 4 were waited for; matrix products, arithmetic and copies ran while one was open for 3% of the time, Pallas kernels for 0%

commit v1 on v0

v1 whole, which is shorter than its diff:
```python
import functools
import math

import jax
import jax.numpy as jnp
from jax import lax
from jax.experimental import pallas as pl
from jax.experimental.pallas import tpu as pltpu
from jax.sharding import PartitionSpec as P

ROWS = 1024
FF = 2048
D = 512
TAU = 64
CHUNK = 256
MESH = pl.DeviceIdType.MESH
NT = (((1,), (1,)), ((), ()))
SCALE2 = math.log2(math.e) / math.sqrt(D)
ORDERS = ("xyz", "yzx", "zxy", "xzy")


def place(x, y, z, c):
    return (x * 4 + (y % 2) * 2 + c, z * 2 + y // 2)


def kernel(
    hidden_hbm, weight_hbm, stamps_ref, ids_ref,
    gh_hbm, gw_ref, tot_ref,
    hid, wgt, ht, emb, mate, zx, aux, theirs, col_u, col_v, col_i, row_u, row_v, row_i,
    acc, summed, coef, sums, psend, precv, part1, part2, part3, got1, got2, got3,
    tsend, tcore, taxis, ghs,
    in_sem, out_sem, aux_send, aux_recv, core_send, core_recv, zx_send, zx_recv,
    p_send, p_recv, s1_send, s1_recv, s2_send, s2_recv, s3_send, s3_recv,
    tc_send, tc_recv, ta_send, ta_recv,
):
    b = lax.axis_index("blk")
    g = lax.axis_index("grp")
    at = {"x": b // 4, "y": (g % 2) * 2 + (b // 2) % 2, "z": g // 2}
    core = b % 2

    def peer(axis, ahead):
        there = dict(at)
        there[axis] = (at[axis] + ahead) % 4
        return place(there["x"], there["y"], there["z"], core)

    core_mate = place(at["x"], at["y"], at["z"], 1 - core)
    partners = (core_mate, peer("z", 2), peer("x", 2))

    def remote(src, dst, send, recv, device):
        return pltpu.make_async_remote_copy(
            src_ref=src, dst_ref=dst, send_sem=send, recv_sem=recv,
            device_id=device, device_id_type=MESH,
        )

    def weight_in():
        return pltpu.make_async_copy(weight_hbm, wgt, in_sem.at[4])

    def hidden_in(i):
        rows = pl.ds(i * CHUNK, CHUNK)
        return pltpu.make_async_copy(hidden_hbm.at[rows], hid.at[rows], in_sem.at[i])

    def grad_out(i):
        rows = pl.ds(i * CHUNK, CHUNK)
        return pltpu.make_async_copy(ghs.at[rows], gh_hbm.at[rows], out_sem.at[i])

    def aux_copy(k):
        return remote(aux, theirs.at[k], aux_send.at[k], aux_recv.at[k], partners[k])

    def core_copy(i):
        rows = pl.ds(i * CHUNK, CHUNK)
        return remote(emb.at[rows], mate.at[rows], core_send.at[i], core_recv.at[i], core_mate)

    def zx_copy(i, k):
        return remote(
            emb.at[pl.ds(i * 128, 128)], zx.at[i, pl.ds(k * 128, 128)],
            zx_send.at[k, i], zx_recv.at[k, i], partners[1 + k],
        )

    def p_copy(i):
        return remote(psend.at[i], precv.at[i], p_send.at[i], p_recv.at[i], core_mate)

    def stage_copy(p, stage, ahead):
        axis = ORDERS[p][stage]
        src, dst, send, recv = (
            (part1, got1, s1_send, s1_recv),
            (part2, got2, s2_send, s2_recv),
            (part3, got3, s3_send, s3_recv),
        )[stage]
        return remote(
            src.at[p, (at[axis] + ahead) % 4], dst.at[p, ahead - 1],
            send.at[p, ahead - 1], recv.at[p, ahead - 1], peer(axis, ahead),
        )

    def total_core():
        return remote(tsend.at[0], tcore, tc_send, tc_recv, core_mate)

    def total_axis(n, ahead):
        axis = "xyz"[n]
        return remote(
            tsend.at[1 + n], taxis.at[n, at[axis]],
            ta_send.at[n, ahead - 1], ta_recv.at[n, ahead - 1], peer(axis, ahead),
        )

    hidden_in(0).start()
    weight_in().start()
    for i in range(1, 4):
        hidden_in(i).start()

    barrier = pltpu.get_barrier_semaphore()
    pl.semaphore_signal(barrier, inc=1, device_id=core_mate, device_id_type=MESH)
    for axis in "xyz":
        for ahead in (1, 2, 3):
            pl.semaphore_signal(barrier, inc=1, device_id=peer(axis, ahead), device_id_type=MESH)

    aux[0] = stamps_ref[...]
    aux[1] = ids_ref[...]

    def columns(k, stamps, ids):
        times = stamps.astype(jnp.float32) * (1.0 / TAU)
        u = jnp.exp(times)
        v = jnp.exp(-times)
        names = ids.astype(jnp.float32)
        col_u[k] = u
        col_v[k] = v
        col_i[k] = names
        return u, v, names

    u, v, names = columns(0, stamps_ref[...], ids_ref[...])
    root = 1.0 / math.sqrt(D)
    for value, rows in zip((u * root, v * root, names), (row_u, row_v, row_i)):
        for r in range(8):
            rows[r * 128 : (r + 1) * 128, :] = jnp.broadcast_to(value[r : r + 1, :], (128, 128)).T
    acc[...] = jnp.zeros_like(acc)
    sums[...] = jnp.zeros_like(sums)

    pl.semaphore_wait(barrier, 10)
    for k in range(3):
        aux_copy(k).start()
    weight_in().wait()

    def embed(i, carry):
        hidden_in(i).wait()
        rows = pl.ds(pl.multiple_of(i * CHUNK, CHUNK), CHUNK)
        emb[rows, :] = jnp.dot(
            hid[rows, :], wgt[...], preferred_element_type=jnp.float32
        ).astype(jnp.bfloat16)
        for h in range(2):
            for k in range(2):
                zx_copy(2 * i + h, k).start()
        core_copy(i).start()
        return carry

    lax.fori_loop(0, 4, embed, 0)

    def pairs(other, cols, diagonal=None):
        loss = jnp.zeros((8, 128), jnp.float32)
        total = jnp.zeros((8, 128), jnp.float32)
        for r in range(4):
            s = lax.dot_general(
                emb[r * CHUNK : (r + 1) * CHUNK, :], other, NT,
                preferred_element_type=jnp.float32,
            )
            for q in range(8):
                lo = r * CHUNK + q * 32
                ru, rv, ri = row_u[lo : lo + 32, :], row_v[lo : lo + 32, :], row_i[lo : lo + 32, :]
                for h in range(2):
                    cu, cv, ci = cols[h]
                    p = s[q * 32 : (q + 1) * 32, h * 128 : (h + 1) * 128] * SCALE2
                    w = jnp.minimum(ru * cv, rv * cu)
                    if diagonal is not None:
                        i = lax.broadcasted_iota(jnp.int32, (32, 128), 0) + lo
                        j = lax.broadcasted_iota(jnp.int32, (32, 128), 1) + (diagonal + h * 128)
                        w = jnp.where(i == j, 0.0, w)
                    same = ri == ci
                    minus = -p
                    e = jnp.exp2(jnp.minimum(p, minus))
                    t = 1.0 + e
                    m = jnp.where(same, minus, p)
                    sig = pl.reciprocal(t, approx=True) * jnp.where(m >= 0.0, 1.0, e)
                    c = w * sig
                    c = jnp.where(same, -c, c)
                    coef[r, q * 32 : (q + 1) * 32, h * 128 : (h + 1) * 128] = c.astype(jnp.bfloat16)
                    term = w * (jnp.maximum(m, 0.0) + jnp.log2(t))
                    for n in range(4):
                        loss = loss + term[n * 8 : (n + 1) * 8]
                        total = total + w[n * 8 : (n + 1) * 8]
            acc[r * CHUNK : (r + 1) * CHUNK, :] += jnp.dot(
                coef[r], other, preferred_element_type=jnp.float32
            )
        sums[0] += total
        sums[1] += loss

    def col_of(k, i):
        return tuple(ref[k, pl.ds(i, 1), :] for ref in (col_u, col_v, col_i))

    def own_step(i, carry):
        rows = pl.ds(pl.multiple_of(i * CHUNK, CHUNK), CHUNK)
        pairs(emb[rows, :], (col_of(0, 2 * i), col_of(0, 2 * i + 1)), i * CHUNK)
        return carry

    lax.fori_loop(0, 4, own_step, 0)

    for k in range(3):
        aux_copy(k).wait_recv()
        columns(1 + k, theirs[k, 0], theirs[k, 1])

    def core_step(i, carry):
        core_copy(i).wait_recv()
        rows = pl.ds(pl.multiple_of(i * CHUNK, CHUNK), CHUNK)
        pairs(mate[rows, :], (col_of(1, 2 * i), col_of(1, 2 * i + 1)))
        return carry

    lax.fori_loop(0, 4, core_step, 0)

    def zx_step(i, carry):
        for c in range(2):
            lanes = pl.ds(pl.multiple_of(i * 256 + c * 128, 128), 128)
            turned = hid[:, lanes].T
            for n in range(8):
                ht[c, i // 2, (n % 2) * 2 + i % 2, n // 2] = turned[n * 16 : (n + 1) * 16, :]
        for k in range(2):
            zx_copy(i, k).wait_recv()
        pairs(zx[i], (col_of(2, i), col_of(3, i)))
        return carry

    lax.fori_loop(0, 8, zx_step, 0)

    summed[...] = acc[...].astype(jnp.bfloat16)

    def p_other(i, carry):
        block = ht[1 - core, i].reshape(CHUNK, ROWS)
        psend[i] = (
            jnp.dot(block, summed[...], preferred_element_type=jnp.float32)
            .astype(jnp.bfloat16)
            .reshape(4, 4, 16, D)
        )
        p_copy(i).start()
        return carry

    lax.fori_loop(0, 4, p_other, 0)

    line = lax.broadcasted_iota(jnp.int32, (8, 128), 0)
    w_sum = jnp.sum(sums[0], axis=0, keepdims=True)
    l_sum = jnp.sum(sums[1], axis=0, keepdims=True)
    tsend[0] = jnp.where(line == 0, w_sum, jnp.where(line == 1, l_sum, 0.0))
    total_core().start()

    def p_own(i, carry):
        block = ht[core, i].reshape(CHUNK, ROWS)
        v = jnp.dot(block, summed[...], preferred_element_type=jnp.float32)
        p_copy(i).wait_recv()
        v = v + precv[i].reshape(CHUNK, D).astype(jnp.float32)
        v = v.astype(jnp.bfloat16).reshape(4, 4, 16, D)
        part1[0, i] = v[..., :128]
        part1[1, :, :, i] = v[..., 128:256]
        for y in range(4):
            part1[2, :, i, y] = v[y, :, :, 256:384]
            part1[3, i, :, y] = v[y, :, :, 384:]
        return carry

    lax.fori_loop(0, 4, p_own, 0)

    for p in range(4):
        for ahead in (2, 1, 3):
            stage_copy(p, 0, ahead).start()
    total_core().wait_recv()

    def spread(n, value):
        tsend[1 + n] = value
        taxis[n, at["xyz"[n]]] = value
        for ahead in (2, 1, 3):
            total_axis(n, ahead).start()

    def gathered(n):
        for ahead in (1, 2, 3):
            total_axis(n, ahead).wait_recv()
        return (taxis[n, 0] + taxis[n, 1]) + (taxis[n, 2] + taxis[n, 3])

    spread(0, tsend[0] + tcore[...])

    def grad_rows(i, carry):
        rows = pl.ds(pl.multiple_of(i * CHUNK, CHUNK), CHUNK)
        for n in range(4):
            ghs[rows, n * 512 : (n + 1) * 512] = lax.dot_general(
                summed[rows, :], wgt[n * 512 : (n + 1) * 512, :], NT,
                preferred_element_type=jnp.float32,
            ).astype(jnp.bfloat16)
        grad_out(i).start()
        return carry

    lax.fori_loop(0, 2, grad_rows, 0)

    def reduced(p, stage):
        src, got = ((part1, got1), (part2, got2), (part3, got3))[stage]
        for ahead in (1, 2, 3):
            stage_copy(p, stage, ahead).wait_recv()
        v = src[p, at[ORDERS[p][stage]]].astype(jnp.float32)
        for n in range(3):
            v = v + got[p, n].astype(jnp.float32)
        return v

    for p in (1, 2, 0, 3):
        part2[p] = reduced(p, 0).astype(jnp.bfloat16)
        for ahead in (2, 1, 3):
            stage_copy(p, 1, ahead).start()
    spread(1, gathered(0))

    lax.fori_loop(2, 3, grad_rows, 0)

    for p in range(4):
        part3[p] = reduced(p, 1).astype(jnp.bfloat16)
        for ahead in (2, 1, 3):
            stage_copy(p, 2, ahead).start()
    spread(2, gathered(1))

    lax.fori_loop(3, 4, grad_rows, 0)

    for p in range(4):
        gw_ref[:, p * 128 : (p + 1) * 128] = reduced(p, 2)
    tot_ref[...] = jnp.broadcast_to(
        jnp.sum(gathered(2), axis=1, keepdims=True), (8, 128)
    )

    for k in range(3):
        aux_copy(k).wait_send()
    for i in range(4):
        core_copy(i).wait_send()
        p_copy(i).wait_send()
        grad_out(i).wait()
    for i in range(8):
        for k in range(2):
            zx_copy(i, k).wait_send()
    total_core().wait_send()
    for ahead in (1, 2, 3):
        for p in range(4):
            for stage in range(3):
                stage_copy(p, stage, ahead).wait_send()
        for n in range(3):
            total_axis(n, ahead).wait_send()


def on_device(hidden, weight, stamps, group_ids):
    device_count = lax.axis_size("blk") * lax.axis_size("grp")
    bf, f32 = jnp.bfloat16, jnp.float32
    sem = pltpu.SemaphoreType.DMA
    vm = pltpu.VMEM
    whole = pl.BlockSpec(memory_space=pl.ANY)
    local = pl.BlockSpec(memory_space=pltpu.VMEM)
    grad, partial, totals = pl.pallas_call(
        kernel,
        out_shape=(
            jax.ShapeDtypeStruct((ROWS, FF), bf),
            jax.ShapeDtypeStruct((16, D), f32),
            jax.ShapeDtypeStruct((8, 128), f32),
        ),
        in_specs=[whole, whole, local, local],
        out_specs=(whole, local, local),
        scratch_shapes=[
            vm((ROWS, FF), bf), vm((FF, D), bf), vm((2, 4, 4, 4, 16, ROWS), bf),
            vm((ROWS, D), bf), vm((ROWS, D), bf), vm((8, CHUNK, D), bf),
            vm((2, 8, 128), jnp.int32), vm((3, 2, 8, 128), jnp.int32),
            vm((4, 8, 128), f32), vm((4, 8, 128), f32), vm((4, 8, 128), f32),
            vm((ROWS, 128), f32), vm((ROWS, 128), f32), vm((ROWS, 128), f32),
            vm((ROWS, D), f32), vm((ROWS, D), bf), vm((4, CHUNK, CHUNK), bf),
            vm((2, 8, 128), f32),
            vm((4, 4, 4, 16, D), bf), vm((4, 4, 4, 16, D), bf),
            vm((4, 4, 4, 4, 16, 128), bf), vm((4, 4, 4, 16, 128), bf), vm((4, 4, 16, 128), bf),
            vm((4, 3, 4, 4, 16, 128), bf), vm((4, 3, 4, 16, 128), bf), vm((4, 3, 16, 128), bf),
            vm((4, 8, 128), f32), vm((8, 128), f32), vm((3, 4, 8, 128), f32),
            vm((ROWS, FF), bf),
            sem((5,)), sem((4,)), sem((3,)), sem((3,)), sem((4,)), sem((4,)),
            sem((2, 8)), sem((2, 8)), sem((4,)), sem((4,)),
            sem((4, 3)), sem((4, 3)), sem((4, 3)), sem((4, 3)), sem((4, 3)), sem((4, 3)),
            sem, sem, sem((3, 3)), sem((3, 3)),
        ],
        compiler_params=pltpu.CompilerParams(
            collective_id=0, has_side_effects=True, vmem_limit_bytes=56 << 20
        ),
        cost_estimate=pl.CostEstimate(
            flops=15 * 10**9, bytes_accessed=11 << 20, transcendentals=12 << 20
        ),
    )(hidden, weight, stamps.reshape(8, 128), group_ids.reshape(8, 128))
    weight_total = (0.5 * math.sqrt(D)) * totals[0, 0]
    pair_loss = (0.5 * math.sqrt(D) * math.log(2.0)) * totals[1, 0]
    pair_count = (
        device_count * ROWS * (ROWS - 1) // 2 + 3 * device_count * ROWS * ROWS // 2
    )
    mean_weight = weight_total / float(pair_count)
    grad_hidden = (grad.astype(f32) / mean_weight).astype(bf)
    grad_weight = partial / (mean_weight * float(device_count * ROWS))
    return grad_hidden, grad_weight, pair_loss / weight_total


def solution(mesh):
    in_specs = (P(("blk", "grp"), None), P(), P(("blk", "grp")), P(("blk", "grp")))
    out_specs = (P(("blk", "grp"), None), P(("blk", "grp"), None), P())
    return jax.shard_map(
        on_device, mesh=mesh, in_specs=in_specs, out_specs=out_specs, check_vma=False
    )
```

time: 796 us -> 73.3 us (0.09)
  waiting for transfers between devices: 630 us -> 0 us
  blocking collectives: 65.2 us -> 0 us
  Pallas kernels: 0 us -> 60.4 us
  matrix products: 32.8 us -> 0 us
  between operations: 23.3 us -> 4.41 us
  starting transfers between devices: 16.7 us -> 0 us
  local copies, waits for them, and re-layouts: 12.4 us -> 1.27 us
  other arithmetic: 15.2 us -> 6.89 us
    unnamed x2 -> x0, waiting for transfers between devices: 565 us -> none
    psum x1 -> x0, blocking collectives: 65.2 us -> none  [on_device(): weight_total, pair_loss = lax.psum((weight_sum, loss_sum), ('blk', 'grp'))]
    ppermute x12 -> x0, waiting for transfers between devices: 64.6 us -> none  [swapped(): lax.ppermute(value, axis, [(i, i ^ 1 << apart) for i in range(lax.axis_si...]
    pallas_call x0 -> x1, Pallas kernels: none -> 60.4 us  [on_device(): pl.pallas_call(kernel, out_shape=(jax.ShapeDtypeStruct((ROWS, FF), bf), j...]
    dot_general x14 -> x0, matrix products: 32.8 us -> none  [the longest x4 9.82 us: pair_terms(): jnp.einsum('...id,...jd->...ij', left_emb, right_emb, preferred_element_t...]
    ppermute x12 -> x0, starting transfers between devices: 16.7 us -> none  [swapped(): lax.ppermute(value, axis, [(i, i ^ 1 << apart) for i in range(lax.axis_si...]
    reduce_sum x1 -> x0, other arithmetic: 8.97 us -> none  [on_device(): loss_sum = loss_sum + jnp.sum(losses)]
  transfers between devices with their start and end apart: 13 -> 0, of which waited for: 4 -> 0; matrix products, arithmetic and copies ran while one was open for 3% -> 0% of each run, Pallas kernels for 0% -> 0%
where the time goes in v1:
time: 73.3 us; the launch traced here: 72.9 us
  Pallas kernels  60.4 us (82%)
  other arithmetic  6.89 us (9%)
  between operations  4.41 us (6%)
  local copies, waits for them, and re-layouts  1.27 us (2%)
    pallas_call x1, Pallas kernels, on_device(): pl.pallas_call(kernel, out_shape=(jax.ShapeDtypeStruct((ROWS, FF), bf), j...  60.4 us
    convert_element_type x1, other arithmetic, on_device(): grad_hidden = (grad.astype(f32) / mean_weight).astype(bf)  5.51 us

profile of v1, /device:TPU:0, one launch (start us, length us, event | category | flops | bytes accessed | tf_op | source)
XLA Modules:
  0.0 72.9 jit_solution(2900231068309907086)
XLA Ops:
  0.6 60.4 %shard_map.67 = (bf16[1024,2048]{1,0:T(8,128)(2,1)}, f32[16,512]{1,0:T(8,128)}, f32[8,128]{1,0:T(8,128)}) custom-call(bf16[1024,2048]{1,0:T(8,128)(2,1)} %hidden_hbm.1, bf16[2048,512]{1,0:T(8,128)(2,1)} %weight_hbm.1, s32[8,128]{1,0:T(8,128)} %bitcast.5, s32[8,128]{1,0:T(8,128)} %bitcast.6), custom_call_target="tpu_custom_call" | custom-call | flops 15000000512 | bytes 11534336 | tf_op jit(solution)/shard_map/pallas_call | solution.py:349
  61.0 1.3 %fusion = (f32[1,1]{1,0:T(1,128)}, f32[1,1]{1,0:T(1,128)}) fusion(f32[8,128]{1,0:T(8,128)} %get-tuple-element.7), kind=kLoop, calls=%fused_computation.2 | loop fusion | bytes 16 | tf_op jit(solution)/shard_map/slice | solution.py:384
  64.3 1.4 %broadcast_divide_fusion = f32[16,512]{1,0:T(8,128)} fusion(f32[16,512]{1,0:T(8,128)} %get-tuple-element.8, f32[]{:T(128)} %bitcast.3), kind=kLoop, calls=%fused_computation.1 | loop fusion | flops 8192 | bytes 65540 | tf_op jit(solution)/shard_map/div | solution.py:390
  66.3 5.5 %divide_convert_fusion = bf16[1024,2048]{1,0:T(8,128)(2,1)} fusion(bf16[1024,2048]{1,0:T(8,128)(2,1)} %get-tuple-element.6, f32[]{:T(128)} %bitcast.2), kind=kLoop, calls=%fused_computation | loop fusion | flops 6291456 | bytes 8388612 | tf_op jit(solution)/shard_map/convert_element_type | solution.py:389

commit v2 on v1

v2 whole, which is shorter than its diff:
```python
import functools
import math

import jax
import jax.numpy as jnp
from jax import lax
from jax.experimental import pallas as pl
from jax.experimental.pallas import tpu as pltpu
from jax.sharding import PartitionSpec as P

ROWS = 1024
FF = 2048
D = 512
TAU = 64
CHUNK = 256
MESH = pl.DeviceIdType.MESH
NT = (((1,), (1,)), ((), ()))
SCALE2 = math.log2(math.e) / math.sqrt(D)
ORDERS = ("xyz", "yzx", "zxy", "mzn")


def place(x, y, z, c):
    return (x * 4 + (y % 2) * 2 + c, z * 2 + y // 2)


def kernel(
    hidden_hbm, weight_hbm, stamps_hbm, ids_hbm,
    gh_ref, gw_ref, tot_ref,
    hid, wgt, ht, htm, emb, aux, theirs, col_u, col_v, col_i, row_u, row_v, row_i,
    acc, summed, coef, coef_last, sums, pown, part1, part2, part3, got1, got2, got3,
    tsend, tcore, taxis,
    in_sem, aux_send, aux_recv, core_send, core_recv, zx_send, zx_recv,
    h_send, h_recv, p_send, p_recv, s1_send, s1_recv, s2_send, s2_recv, s3_send, s3_recv,
    tc_send, tc_recv, ta_send, ta_recv,
):
    b = lax.axis_index("blk")
    g = lax.axis_index("grp")
    at = {"x": b // 4, "y": (g % 2) * 2 + (b // 2) % 2, "z": g // 2}
    core = b % 2

    at["m"] = at["x"] * (1 - core) + at["y"] * core
    at["n"] = at["y"] * (1 - core) + at["x"] * core

    def peer(axis, ahead):
        steps = {
            "x": (ahead, 0, 0), "y": (0, ahead, 0), "z": (0, 0, ahead),
            "m": (ahead * (1 - core), ahead * core, 0),
            "n": (ahead * core, ahead * (1 - core), 0),
        }[axis]
        there = [(at[a] + step) % 4 for a, step in zip("xyz", steps)]
        return place(*there, core)

    core_mate = place(at["x"], at["y"], at["z"], 1 - core)
    partners = (core_mate, peer("z", 2), peer("x", 2))

    def remote(src, dst, send, recv, device):
        return pltpu.make_async_remote_copy(
            src_ref=src, dst_ref=dst, send_sem=send, recv_sem=recv,
            device_id=device, device_id_type=MESH,
        )

    def weight_in():
        return pltpu.make_async_copy(weight_hbm, wgt, in_sem.at[8])

    def hidden_in(i):
        rows = pl.ds(i * 128, 128)
        return pltpu.make_async_copy(hidden_hbm.at[rows], hid.at[rows], in_sem.at[i])

    def aux_in(k):
        return pltpu.make_async_copy((stamps_hbm, ids_hbm)[k], aux.at[k], in_sem.at[9 + k])

    def aux_copy(k):
        return remote(aux, theirs.at[k], aux_send.at[k], aux_recv.at[k], partners[k])

    def core_copy(i):
        return remote(
            emb.at[pl.ds(i * CHUNK, CHUNK)], emb.at[pl.ds(ROWS + i * CHUNK, CHUNK)],
            core_send.at[i], core_recv.at[i], core_mate,
        )

    def zx_copy(i, k):
        return remote(
            emb.at[pl.ds(i * 128, 128)], emb.at[pl.ds(2 * ROWS + i * CHUNK + k * 128, 128)],
            zx_send.at[k, i], zx_recv.at[k, i], partners[1 + k],
        )

    def h_copy(i):
        return remote(ht.at[1 - core, i], htm.at[i], h_send.at[i], h_recv.at[i], core_mate)

    def p_copy(i):
        rows = pl.ds(i * CHUNK, CHUNK)
        return remote(
            summed.at[0, rows], summed.at[1, rows], p_send.at[i], p_recv.at[i], core_mate
        )

    def stage_copy(p, stage, ahead):
        axis = ORDERS[p][stage]
        src, dst, send, recv = (
            (part1, got1, s1_send, s1_recv),
            (part2, got2, s2_send, s2_recv),
            (part3, got3, s3_send, s3_recv),
        )[stage]
        return remote(
            src.at[p, (at[axis] + ahead) % 4], dst.at[p, ahead - 1],
            send.at[p, ahead - 1], recv.at[p, ahead - 1], peer(axis, ahead),
        )

    def total_core():
        return remote(tsend.at[0], tcore, tc_send, tc_recv, core_mate)

    def total_axis(n, ahead):
        axis = "xyz"[n]
        return remote(
            tsend.at[1 + n], taxis.at[n, at[axis]],
            ta_send.at[n, ahead - 1], ta_recv.at[n, ahead - 1], peer(axis, ahead),
        )

    for k in range(2):
        aux_in(k).start()
    weight_in().start()
    for i in range(8):
        hidden_in(i).start()

    barrier = pltpu.get_barrier_semaphore()
    pl.semaphore_signal(barrier, inc=1, device_id=core_mate, device_id_type=MESH)
    for axis in "zxy":
        for ahead in (2, 1, 3):
            pl.semaphore_signal(barrier, inc=1, device_id=peer(axis, ahead), device_id_type=MESH)

    weight_in().wait()

    def embed(first, count):
        for n in range(count // 128):
            hidden_in(first // 128 + n).wait()
        rows = pl.ds(first, count)
        emb[rows, :] = jnp.dot(
            hid[rows, :], wgt[...], preferred_element_type=jnp.float32
        ).astype(jnp.bfloat16)

    embed(0, 128)
    pl.semaphore_wait(barrier, 10)
    for k in range(2):
        zx_copy(0, k).start()
    for k in range(2):
        aux_in(k).wait()
    for k in range(3):
        aux_copy(k).start()
    embed(128, 128)
    for k in range(2):
        zx_copy(1, k).start()
    core_copy(0).start()

    def embed_rest(i, carry):
        embed(pl.multiple_of(i * CHUNK, CHUNK), CHUNK)
        for h in range(2):
            for k in range(2):
                zx_copy(2 * i + h, k).start()
        core_copy(i).start()
        return carry

    lax.fori_loop(1, 4, embed_rest, 0)

    def columns(place_of, stamps, ids):
        times = stamps.astype(jnp.float32) * (1.0 / TAU)
        values = (jnp.exp(times), jnp.exp(-times), ids.astype(jnp.float32))
        for value, ref in zip(values, (col_u, col_v, col_i)):
            for r in range(8):
                ref[place_of(r) : place_of(r) + 1, :] = value[r : r + 1, :]
        return values

    u, v, names = columns(lambda r: r, aux[0], aux[1])
    ln2 = math.log(2.0)
    for value, rows in zip((u * ln2, v * ln2, names), (row_u, row_v, row_i)):
        for r in range(8):
            rows[r * 128 : (r + 1) * 128, :] = jnp.broadcast_to(value[r : r + 1, :], (128, 128)).T
    acc[...] = jnp.zeros_like(acc)
    sums[...] = jnp.zeros_like(sums)

    def pairs(first, width, coef, diagonal=False, last=False):
        other = emb[pl.ds(pl.multiple_of(first, width), width), :]
        cols = [
            [ref[pl.ds(first // 128 + h, 1), :] for ref in (col_u, col_v, col_i)]
            for h in range(width // 128)
        ]
        loss = jnp.zeros((8, 128), jnp.float32)
        total = jnp.zeros((8, 128), jnp.float32)

        def scores(r):
            return lax.dot_general(
                emb[r * CHUNK : (r + 1) * CHUNK, :], other, NT,
                preferred_element_type=jnp.float32,
            )

        def gather(r):
            rows = slice(r * CHUNK, (r + 1) * CHUNK)
            v = acc[rows, :] + jnp.dot(coef[rows, :], other, preferred_element_type=jnp.float32)
            if last:
                summed[0, rows, :] = v.astype(jnp.bfloat16)
                p_copy(r).start()
            else:
                acc[rows, :] = v

        s = scores(0)
        for r in range(4):
            s_next = scores(r + 1) if r < 3 else None
            if r > 0:
                gather(r - 1)
            for q in range(8):
                lo = r * CHUNK + q * 32
                ru, rv, ri = row_u[lo : lo + 32, :], row_v[lo : lo + 32, :], row_i[lo : lo + 32, :]
                for h in range(width // 128):
                    cu, cv, ci = cols[h]
                    sign = jnp.where(ri == ci, -SCALE2, SCALE2)
                    m = s[q * 32 : (q + 1) * 32, h * 128 : (h + 1) * 128] * sign
                    plus = jnp.maximum(m, jnp.log2(1.0 + jnp.exp2(jnp.minimum(m, 100.0))))
                    w = jnp.minimum(ru * cv, rv * cu)
                    if diagonal:
                        i = lax.broadcasted_iota(jnp.int32, (32, 128), 0) + lo
                        j = lax.broadcasted_iota(jnp.int32, (32, 128), 1) + (first + h * 128)
                        w = jnp.where(i == j, 0.0, w)
                    c = (w * sign) * jnp.exp2(m - plus)
                    coef[lo : lo + 32, h * 128 : (h + 1) * 128] = c.astype(jnp.bfloat16)
                    term = w * plus
                    for n in range(4):
                        loss = loss + term[n * 8 : (n + 1) * 8]
                        total = total + w[n * 8 : (n + 1) * 8]
            s = s_next
        gather(3)
        sums[0] += total
        sums[1] += loss

    def own_step(i, carry):
        pairs(i * 512, 512, coef, True)
        return carry

    lax.fori_loop(0, 2, own_step, 0)

    for k in range(3):
        aux_copy(k).wait_recv()
    columns(lambda r: 8 + r, theirs[0, 0], theirs[0, 1])
    columns(lambda r: 16 + 2 * r, theirs[1, 0], theirs[1, 1])
    columns(lambda r: 17 + 2 * r, theirs[2, 0], theirs[2, 1])

    def turn(x, carry):
        for n in range(4):
            lanes = pl.ds(pl.multiple_of(x * 512 + n * 128, 128), 128)
            turned = hid[:, lanes].T
            for k in range(8):
                ht[n % 2, x, (k % 2) * 2 + n // 2, k // 2] = turned[k * 16 : (k + 1) * 16, :]
        h_copy(x).start()
        return carry

    def other_step(i, carry):
        @pl.when(i < 2)
        def _():
            for n in range(2):
                core_copy(2 * i + n).wait_recv()

        @pl.when(i == 2)
        def _():
            lax.fori_loop(0, 4, turn, 0)

        @pl.when(i >= 2)
        def _():
            for n in range(2):
                for k in range(2):
                    zx_copy(2 * (i - 2) + n, k).wait_recv()

        pairs(ROWS + i * 512, 512, coef)
        return carry

    lax.fori_loop(0, 5, other_step, 0)

    for i in (6, 7):
        for k in range(2):
            zx_copy(i, k).wait_recv()
        pairs(2 * ROWS + i * CHUNK, CHUNK, coef_last, last=i == 7)

    line = lax.broadcasted_iota(jnp.int32, (8, 128), 0)
    w_sum = jnp.sum(sums[0], axis=0, keepdims=True)
    l_sum = jnp.sum(sums[1], axis=0, keepdims=True)
    tsend[0] = jnp.where(line == 0, w_sum, jnp.where(line == 1, l_sum, 0.0))
    total_core().start()

    def own_half(x, carry):
        block = ht[core, x].reshape(CHUNK, ROWS)
        pown[x] = jnp.dot(block, summed[0], preferred_element_type=jnp.float32)
        return carry

    lax.fori_loop(0, 4, own_half, 0)
    for i in range(4):
        h_copy(i).wait_recv()
        p_copy(i).wait_recv()

    def mate_half(pair):
        lanes = slice(pair * 256, (pair + 1) * 256)

        def step(x, carry):
            block = htm[x].reshape(CHUNK, ROWS)
            v = pown[x, :, lanes] + jnp.dot(
                block, summed[1, :, lanes], preferred_element_type=jnp.float32
            )
            v = v.astype(jnp.bfloat16).reshape(4, 4, 16, 256)
            if pair == 0:
                part1[0, x] = v[..., :128]
                part1[1, :, :, x] = v[..., 128:]
            else:
                for y in range(4):
                    part1[2, :, x, y] = v[y, :, :, :128]
                    m = x * (1 - core) + y * core
                    n = y * (1 - core) + x * core
                    part1[3, m, :, n] = v[y, :, :, 128:]
            return carry

        lax.fori_loop(0, 4, step, 0)
        for p in (2 * pair, 2 * pair + 1):
            for ahead in (2, 1, 3):
                stage_copy(p, 0, ahead).start()

    mate_half(0)
    mate_half(1)
    total_core().wait_recv()

    def spread(n, value):
        tsend[1 + n] = value
        taxis[n, at["xyz"[n]]] = value
        for ahead in (2, 1, 3):
            total_axis(n, ahead).start()

    def gathered(n):
        for ahead in (1, 2, 3):
            total_axis(n, ahead).wait_recv()
        return (taxis[n, 0] + taxis[n, 1]) + (taxis[n, 2] + taxis[n, 3])

    spread(0, tsend[0] + tcore[...])

    def grad_rows(i, carry):
        rows = pl.ds(pl.multiple_of(i * CHUNK, CHUNK), CHUNK)
        for n in range(4):
            gh_ref[rows, n * 512 : (n + 1) * 512] = lax.dot_general(
                summed[0, rows, :], wgt[n * 512 : (n + 1) * 512, :], NT,
                preferred_element_type=jnp.float32,
            ).astype(jnp.bfloat16)
        return carry

    lax.fori_loop(0, 4, grad_rows, 0)

    for k in range(3):
        aux_copy(k).wait_send()
    for i in range(4):
        core_copy(i).wait_send()
        h_copy(i).wait_send()
        p_copy(i).wait_send()
    for i in range(8):
        for k in range(2):
            zx_copy(i, k).wait_send()
    total_core().wait_send()

    def sent(stage):
        for ahead in (1, 2, 3):
            for p in range(4):
                stage_copy(p, stage, ahead).wait_send()
            total_axis(stage, ahead).wait_send()

    def reduced(p, stage):
        src, got = ((part1, got1), (part2, got2), (part3, got3))[stage]
        for ahead in (1, 2, 3):
            stage_copy(p, stage, ahead).wait_recv()
        v = src[p, at[ORDERS[p][stage]]].astype(jnp.float32)
        for n in range(3):
            v = v + got[p, n].astype(jnp.float32)
        return v

    for p in range(4):
        part2[p] = reduced(p, 0).astype(jnp.bfloat16)
        for ahead in (2, 1, 3):
            stage_copy(p, 1, ahead).start()
    spread(1, gathered(0))
    sent(0)

    for p in range(4):
        part3[p] = reduced(p, 1).astype(jnp.bfloat16)
        for ahead in (2, 1, 3):
            stage_copy(p, 2, ahead).start()
    spread(2, gathered(1))
    sent(1)

    for p in range(4):
        gw_ref[:, p * 128 : (p + 1) * 128] = reduced(p, 2)
    tot_ref[...] = jnp.broadcast_to(
        jnp.sum(gathered(2), axis=1, keepdims=True), (8, 128)
    )

    for ahead in (1, 2, 3):
        for p in range(4):
            stage_copy(p, 2, ahead).wait_send()
        total_axis(2, ahead).wait_send()


def scale_kernel(pair_count, items, gh_ref, gw_ref, tot_ref, gh_out, gw_out, loss_out, buf, sem):
    scale = 1.0 / math.log(2.0)
    totals = tot_ref[...]
    weight_total = totals[0:1, :] * (0.5 * scale)
    pair_loss = totals[1:2, :] * 0.5
    inverse = float(pair_count) / weight_total
    across = jnp.broadcast_to(jnp.concatenate([inverse] * 16, axis=1), (8, FF))

    def out(i):
        rows = pl.ds(i * 128, 128)
        return pltpu.make_async_copy(buf.at[rows], gh_out.at[rows], sem.at[i])

    for i in range(8):
        for n in range(8):
            rows = slice(i * 128 + n * 16, i * 128 + (n + 1) * 16)
            v = gh_ref[rows, :].astype(jnp.float32) * jnp.concatenate([across] * 2, axis=0)
            buf[rows, :] = v.astype(jnp.bfloat16)
        out(i).start()
    gw_out[...] = gw_ref[...] * (across[0:1, :D] * (1.0 / items))
    loss_out[...] = (pair_loss / weight_total)[:, 0:1]
    for i in range(8):
        out(i).wait()


def on_device(hidden, weight, stamps, group_ids):
    device_count = lax.axis_size("blk") * lax.axis_size("grp")
    bf, f32 = jnp.bfloat16, jnp.float32
    sem = pltpu.SemaphoreType.DMA
    vm = pltpu.VMEM
    whole = pl.BlockSpec(memory_space=pl.ANY)
    outside = pl.BlockSpec(memory_space=pltpu.HBM)
    local = pl.BlockSpec(memory_space=pltpu.VMEM)
    grad, partial, totals = pl.pallas_call(
        kernel,
        out_shape=(
            pltpu.VMEM((ROWS, FF), bf),
            pltpu.VMEM((16, D), f32),
            pltpu.VMEM((8, 128), f32),
        ),
        in_specs=[outside] * 4,
        out_specs=(local, local, local),
        scratch_shapes=[
            vm((ROWS, FF), bf), vm((FF, D), bf), vm((2, 4, 4, 4, 16, ROWS), bf),
            vm((4, 4, 4, 16, ROWS), bf), vm((4 * ROWS, D), bf),
            vm((2, 8, 128), jnp.int32), vm((3, 2, 8, 128), jnp.int32),
            vm((32, 128), f32), vm((32, 128), f32), vm((32, 128), f32),
            vm((ROWS, 128), f32), vm((ROWS, 128), f32), vm((ROWS, 128), f32),
            vm((ROWS, D), f32), vm((2, ROWS, D), bf), vm((ROWS, 512), bf), vm((ROWS, CHUNK), bf),
            vm((2, 8, 128), f32), vm((4, CHUNK, D), f32),
            vm((4, 4, 4, 4, 16, 128), bf), vm((4, 4, 4, 16, 128), bf), vm((4, 4, 16, 128), bf),
            vm((4, 3, 4, 4, 16, 128), bf), vm((4, 3, 4, 16, 128), bf), vm((4, 3, 16, 128), bf),
            vm((4, 8, 128), f32), vm((8, 128), f32), vm((3, 4, 8, 128), f32),
            sem((11,)), sem((3,)), sem((3,)), sem((4,)), sem((4,)),
            sem((2, 8)), sem((2, 8)), sem((4,)), sem((4,)), sem((4,)), sem((4,)),
            sem((4, 3)), sem((4, 3)), sem((4, 3)), sem((4, 3)), sem((4, 3)), sem((4, 3)),
            sem, sem, sem((3, 3)), sem((3, 3)),
        ],
        compiler_params=pltpu.CompilerParams(
            collective_id=0, has_side_effects=True, vmem_limit_bytes=44 << 20
        ),
        cost_estimate=pl.CostEstimate(
            flops=15 * 10**9, bytes_accessed=7 << 20, transcendentals=12 << 20
        ),
    )(*(
        pltpu.with_memory_space_constraint(value, pltpu.HBM)
        for value in (hidden, weight, stamps.reshape(8, 128), group_ids.reshape(8, 128))
    ))
    items = device_count * ROWS
    pair_count = items * (ROWS - 1) // 2 + 3 * items * ROWS // 2
    grad_hidden, grad_weight, loss = pl.pallas_call(
        functools.partial(scale_kernel, pair_count, items),
        out_shape=(
            jax.ShapeDtypeStruct((ROWS, FF), bf),
            jax.ShapeDtypeStruct((16, D), f32),
            jax.ShapeDtypeStruct((1, 1), f32),
        ),
        in_specs=[local, local, local],
        out_specs=(whole, local, local),
        scratch_shapes=[vm((ROWS, FF), bf), sem((8,))],
        compiler_params=pltpu.CompilerParams(vmem_limit_bytes=16 << 20),
        cost_estimate=pl.CostEstimate(
            flops=2 << 20, bytes_accessed=4 << 20, transcendentals=0
        ),
    )(grad, partial, totals)
    return grad_hidden, grad_weight, loss[0, 0]


def solution(mesh):
    in_specs = (P(("blk", "grp"), None), P(), P(("blk", "grp")), P(("blk", "grp")))
    out_specs = (P(("blk", "grp"), None), P(("blk", "grp"), None), P())
    return jax.shard_map(
        on_device, mesh=mesh, in_specs=in_specs, out_specs=out_specs, check_vma=False
    )
```

time: 73.3 us -> 55.6 us (0.76)
  other arithmetic: 6.89 us -> 0 us
  Pallas kernels: 60.4 us -> 54.8 us
  between operations: 4.41 us -> 0.64 us
  local copies, waits for them, and re-layouts: 1.27 us -> 0 us
    pallas_call x1 -> x2, Pallas kernels: 60.4 us -> 54.8 us  [the longest x1 52 us: on_device(): pl.pallas_call(kernel, out_shape=(pltpu.VMEM((ROWS, FF), bf), pltpu.VMEM(...]
    convert_element_type x1 -> x0, other arithmetic: 5.51 us -> none  [on_device(): grad_hidden = (grad.astype(f32) / mean_weight).astype(bf)]
    div x1 -> x0, other arithmetic: 1.38 us -> none  [on_device(): grad_weight = partial / (mean_weight * float(device_count * ROWS))]
    slice x1 -> x0, local copies, waits for them, and re-layouts: 1.27 us -> none  [on_device(): pair_loss = 0.5 * math.sqrt(D) * math.log(2.0) * totals[1, 0]]
where the time goes in v2:
time: 55.6 us; the launch traced here: 55.4 us
  Pallas kernels  54.8 us (99%)
  between operations  0.64 us (1%)
    pallas_call x1, Pallas kernels, on_device(): pl.pallas_call(kernel, out_shape=(pltpu.VMEM((ROWS, FF), bf), pltpu.VMEM(...  52 us
    pallas_call x1, Pallas kernels, on_device(): pl.pallas_call(functools.partial(scale_kernel, pair_count, items), out_sh...  2.78 us

profile of v2, /device:TPU:0, one launch (start us, length us, event | category | flops | bytes accessed | tf_op | source)
XLA Modules:
  0.0 55.4 jit_solution(14720638631267102579)
XLA Ops:
  0.6 52.0 %shard_map.67 = (bf16[1024,2048]{1,0:T(8,128)(2,1)S(1)}, f32[16,512]{1,0:T(8,128)S(1)}, f32[8,128]{1,0:T(8,128)S(1)}) custom-call(bf16[1024,2048]{1,0:T(8,128)(2,1)} %hidden_hbm.1, bf16[2048,512]{1,0:T(8,128)(2,1)} %weight_hbm.1, s32[8,128]{1,0:T(8,128)} %bitcast.3, s32[8,128]{1,0:T(8,128)} %bitcast.4), custom_call_target="tpu_custom_call" | custom-call | flops 15000000512 | bytes 7340032 | tf_op jit(solution)/shard_map/pallas_call | solution.py:432
  52.7 2.8 %shard_map.68 = (bf16[1024,2048]{1,0:T(8,128)(2,1)}, f32[16,512]{1,0:T(8,128)}, f32[1,1]{1,0:T(1,128)}) custom-call(bf16[1024,2048]{1,0:T(8,128)(2,1)S(1)} %get-tuple-element.9.gh_ref, f32[16,512]{1,0:T(8,128)S(1)} %get-tuple-element.10.gw_ref, f32[8,128]{1,0:T(8,128)S(1)} %get-tuple-element.11.tot_ref), custom_call_target="tpu_custom_call" | custom-call | flops 2097152 | bytes 4194304 | tf_op jit(solution)/shard_map/pallas_call | solution.py:469

commit v3 on v2

--- a/solution.py
+++ b/solution.py
@@ -15,8 +15,9 @@
 CHUNK = 256
 MESH = pl.DeviceIdType.MESH
 NT = (((1,), (1,)), ((), ()))
+TN = (((0,), (0,)), ((), ()))
 SCALE2 = math.log2(math.e) / math.sqrt(D)
-ORDERS = ("xyz", "yzx", "zxy", "mzn")
+ORDERS = ("zxy", "yzx", "xyz", "mxn")
 
 
 def place(x, y, z, c):
@@ -27,9 +28,10 @@
     hidden_hbm, weight_hbm, stamps_hbm, ids_hbm,
     gh_ref, gw_ref, tot_ref,
     hid, wgt, ht, htm, emb, aux, theirs, col_u, col_v, col_i, row_u, row_v, row_i,
-    acc, summed, coef, coef_last, sums, pown, part1, part2, part3, got1, got2, got3,
+    acc, summed, coef, coef_last, coef_end, sums, pown, part1, part2, part3, got1, got2, got3,
     tsend, tcore, taxis,
     in_sem, aux_send, aux_recv, core_send, core_recv, zx_send, zx_recv,
+    f_send, f_recv, e_send, e_recv,
     h_send, h_recv, p_send, p_recv, s1_send, s1_recv, s2_send, s2_recv, s3_send, s3_recv,
     tc_send, tc_recv, ta_send, ta_recv,
 ):
@@ -38,14 +40,14 @@
     at = {"x": b // 4, "y": (g % 2) * 2 + (b // 2) % 2, "z": g // 2}
     core = b % 2
 
-    at["m"] = at["x"] * (1 - core) + at["y"] * core
-    at["n"] = at["y"] * (1 - core) + at["x"] * core
+    at["m"] = at["z"] * (1 - core) + at["y"] * core
+    at["n"] = at["y"] * (1 - core) + at["z"] * core
 
     def peer(axis, ahead):
         steps = {
             "x": (ahead, 0, 0), "y": (0, ahead, 0), "z": (0, 0, ahead),
-            "m": (ahead * (1 - core), ahead * core, 0),
-            "n": (ahead * core, ahead * (1 - core), 0),
+            "m": (0, ahead * core, ahead * (1 - core)),
+            "n": (0, ahead * (1 - core), ahead * core),
         }[axis]
         there = [(at[a] + step) % 4 for a, step in zip("xyz", steps)]
         return place(*there, core)
@@ -59,8 +61,11 @@
             device_id=device, device_id_type=MESH,
         )
 
-    def weight_in():
-        return pltpu.make_async_copy(weight_hbm, wgt, in_sem.at[8])
+    def weight_in(i):
+        lanes = pl.ds(i * 128, 128)
+        return pltpu.make_async_copy(
+            weight_hbm.at[:, lanes], wgt.at[:, lanes], in_sem.at[11 + i]
+        )
 
     def hidden_in(i):
         rows = pl.ds(i * 128, 128)
@@ -78,10 +83,24 @@
             core_send.at[i], core_recv.at[i], core_mate,
         )
 
+    def end_copy(n, k):
+        return remote(
+            emb.at[pl.ds(896 + n * 64, 64)],
+            emb.at[pl.ds(4 * ROWS - CHUNK + n * 128 + k * 64, 64)],
+            e_send.at[k, n], e_recv.at[k, n], partners[1 + k],
+        )
+
     def zx_copy(i, k):
         return remote(
             emb.at[pl.ds(i * 128, 128)], emb.at[pl.ds(2 * ROWS + i * CHUNK + k * 128, 128)],
             zx_send.at[k, i], zx_recv.at[k, i], partners[1 + k],
+        )
+
+    def first_copy(n, k):
+        lanes = pl.ds(n * 128, 128)
+        return remote(
+            emb.at[pl.ds(0, 128), lanes], emb.at[pl.ds(2 * ROWS + k * 128, 128), lanes],
+            f_send.at[k, n], f_recv.at[k, n], partners[1 + k],
         )
 
     def h_copy(i):
@@ -115,19 +134,21 @@
             ta_send.at[n, ahead - 1], ta_recv.at[n, ahead - 1], peer(axis, ahead),
         )
 
+    barrier = pltpu.get_barrier_semaphore()
+    for device in partners[1:]:
+        pl.semaphore_signal(barrier, inc=1, device_id=device, device_id_type=MESH)
+    hidden_in(0).start()
+    weight_in(0).start()
+    pl.semaphore_signal(barrier, inc=1, device_id=core_mate, device_id_type=MESH)
+    for axis in "zxy":
+        for ahead in (1, 3) if axis != "y" else (2, 1, 3):
+            pl.semaphore_signal(barrier, inc=1, device_id=peer(axis, ahead), device_id_type=MESH)
+    for i in range(1, 4):
+        weight_in(i).start()
     for k in range(2):
         aux_in(k).start()
-    weight_in().start()
-    for i in range(8):
+    for i in range(1, 8):
         hidden_in(i).start()
-
-    barrier = pltpu.get_barrier_semaphore()
-    pl.semaphore_signal(barrier, inc=1, device_id=core_mate, device_id_type=MESH)
-    for axis in "zxy":
-        for ahead in (2, 1, 3):
-            pl.semaphore_signal(barrier, inc=1, device_id=peer(axis, ahead), device_id_type=MESH)
-
-    weight_in().wait()
 
     def embed(first, count):
         for n in range(count // 128):
@@ -137,10 +158,17 @@
             hid[rows, :], wgt[...], preferred_element_type=jnp.float32
         ).astype(jnp.bfloat16)
 
-    embed(0, 128)
-    pl.semaphore_wait(barrier, 10)
-    for k in range(2):
-        zx_copy(0, k).start()
+    hidden_in(0).wait()
+    for n in range(4):
+        lanes = slice(n * 128, (n + 1) * 128)
+        weight_in(n).wait()
+        emb[:128, lanes] = jnp.dot(
+            hid[:128, :], wgt[:, lanes], preferred_element_type=jnp.float32
+        ).astype(jnp.bfloat16)
+        if n == 0:
+            pl.semaphore_wait(barrier, 10)
+        for k in range(2):
+            first_copy(n, k).start()
     for k in range(2):
         aux_in(k).wait()
     for k in range(3):
@@ -158,7 +186,14 @@
         core_copy(i).start()
         return carry
 
-    lax.fori_loop(1, 4, embed_rest, 0)
+    lax.fori_loop(1, 3, embed_rest, 0)
+    embed(768, CHUNK)
+    for k in range(2):
+        zx_copy(6, k).start()
+    for n in range(2):
+        for k in range(2):
+            end_copy(n, k).start()
+    core_copy(3).start()
 
     def columns(place_of, stamps, ids):
         times = stamps.astype(jnp.float32) * (1.0 / TAU)
@@ -170,43 +205,66 @@
 
     u, v, names = columns(lambda r: r, aux[0], aux[1])
     ln2 = math.log(2.0)
-    for value, rows in zip((u * ln2, v * ln2, names), (row_u, row_v, row_i)):
+    stack = jnp.concatenate(
+        [u * ln2, v * ln2, names, jnp.zeros((104, 128), jnp.float32)], axis=0
+    ).T
+    for k, rows in enumerate((row_u, row_v, row_i)):
         for r in range(8):
-            rows[r * 128 : (r + 1) * 128, :] = jnp.broadcast_to(value[r : r + 1, :], (128, 128)).T
+            column = stack[:, k * 8 + r : k * 8 + r + 1]
+            rows[r * 128 : (r + 1) * 128, :] = jnp.broadcast_to(column, (128, 128))
     acc[...] = jnp.zeros_like(acc)
     sums[...] = jnp.zeros_like(sums)
 
-    def pairs(first, width, coef, diagonal=False, last=False):
-        other = emb[pl.ds(pl.multiple_of(first, width), width), :]
-        cols = [
-            [ref[pl.ds(first // 128 + h, 1), :] for ref in (col_u, col_v, col_i)]
-            for h in range(width // 128)
-        ]
-        loss = jnp.zeros((8, 128), jnp.float32)
-        total = jnp.zeros((8, 128), jnp.float32)
-
-        def scores(r):
+    def sweep(tiles, width, coef, last=False):
+        sides = {}
+        for _, first, _, _ in tiles:
+            if id(first) not in sides:
+                sides[id(first)] = (
+                    emb[pl.ds(pl.multiple_of(first, width), width), :],
+                    [
+                        [ref[pl.ds(first // 128 + h, 1), :] for ref in (col_u, col_v, col_i)]
+                        for h in range(width // 128)
+                    ],
+                )
+        loss = [jnp.zeros((8, 128), jnp.float32), jnp.zeros((8, 128), jnp.float32)]
+        total = [jnp.zeros((8, 128), jnp.float32), jnp.zeros((8, 128), jnp.float32)]
+
+        def scores(tile):
+            r, first = tile[:2]
             return lax.dot_general(
-                emb[r * CHUNK : (r + 1) * CHUNK, :], other, NT,
+                emb[r * CHUNK : (r + 1) * CHUNK, :], sides[id(first)][0], NT,
                 preferred_element_type=jnp.float32,
             )
 
-        def gather(r):
+        def gather(t):
+            r, first, _, mirror = tiles[t]
             rows = slice(r * CHUNK, (r + 1) * CHUNK)
-            v = acc[rows, :] + jnp.dot(coef[rows, :], other, preferred_element_type=jnp.float32)
+            held = coef[t % 4 * CHUNK : (t % 4 + 1) * CHUNK, :]
+            v = acc[rows, :] + jnp.dot(
+                held, sides[id(first)][0], preferred_element_type=jnp.float32
+            )
             if last:
                 summed[0, rows, :] = v.astype(jnp.bfloat16)
                 p_copy(r).start()
+                if r == 1:
+                    own_half(0)
             else:
                 acc[rows, :] = v
-
-        s = scores(0)
-        for r in range(4):
-            s_next = scores(r + 1) if r < 3 else None
-            if r > 0:
-                gather(r - 1)
+            if mirror:
+                there = slice(first, first + width)
+                acc[there, :] += lax.dot_general(
+                    held, emb[rows, :], TN, preferred_element_type=jnp.float32
+                )
+
+        s = scores(tiles[0])
+        for t, (r, first, diagonal, mirror) in enumerate(tiles):
+            s_next = scores(tiles[t + 1]) if t + 1 < len(tiles) else None
+            if t > 0:
+                gather(t - 1)
+            cols = sides[id(first)][1]
             for q in range(8):
                 lo = r * CHUNK + q * 32
+                at_coef = t % 4 * CHUNK + q * 32
                 ru, rv, ri = row_u[lo : lo + 32, :], row_v[lo : lo + 32, :], row_i[lo : lo + 32, :]
                 for h in range(width // 128):
                     cu, cv, ci = cols[h]
@@ -214,32 +272,46 @@
                     m = s[q * 32 : (q + 1) * 32, h * 128 : (h + 1) * 128] * sign
                     plus = jnp.maximum(m, jnp.log2(1.0 + jnp.exp2(jnp.minimum(m, 100.0))))
                     w = jnp.minimum(ru * cv, rv * cu)
-                    if diagonal:
-                        i = lax.broadcasted_iota(jnp.int32, (32, 128), 0) + lo
-                        j = lax.broadcasted_iota(jnp.int32, (32, 128), 1) + (first + h * 128)
+                    if diagonal and lo // 128 == first // 128 + h:
+                        i = lax.broadcasted_iota(jnp.int32, (32, 128), 0) + lo % 128
+                        j = lax.broadcasted_iota(jnp.int32, (32, 128), 1)
                         w = jnp.where(i == j, 0.0, w)
                     c = (w * sign) * jnp.exp2(m - plus)
-                    coef[lo : lo + 32, h * 128 : (h + 1) * 128] = c.astype(jnp.bfloat16)
+                    coef[at_coef : at_coef + 32, h * 128 : (h + 1) * 128] = c.astype(jnp.bfloat16)
                     term = w * plus
                     for n in range(4):
-                        loss = loss + term[n * 8 : (n + 1) * 8]
-                        total = total + w[n * 8 : (n + 1) * 8]
+                        loss[mirror] = loss[mirror] + term[n * 8 : (n + 1) * 8]
+                        total[mirror] = total[mirror] + w[n * 8 : (n + 1) * 8]
             s = s_next
-        gather(3)
-        sums[0] += total
-        sums[1] += loss
-
-    def own_step(i, carry):
-        pairs(i * 512, 512, coef, True)
-        return carry
-
-    lax.fori_loop(0, 2, own_step, 0)
+        gather(len(tiles) - 1)
+        sums[0] += total[0] + 2.0 * total[1]
+        sums[1] += loss[0] + 2.0 * loss[1]
+
+    def own_half(k):
+        depth = slice(k * 512, (k + 1) * 512)
+        for x in range(4):
+            block = ht[core, x, :, :, :, depth].reshape(CHUNK, 512)
+            v = jnp.dot(block, summed[0, depth, :], preferred_element_type=jnp.float32)
+            if k:
+                v = v + pown[x]
+            pown[x] = v
+
+    low, high = 0, 512
+    sweep(
+        [(0, low, True, False), (1, low, True, False), (0, high, False, True),
+         (1, high, False, True), (2, high, True, False), (3, high, True, False)],
+        512, coef,
+    )
 
     for k in range(3):
         aux_copy(k).wait_recv()
     columns(lambda r: 8 + r, theirs[0, 0], theirs[0, 1])
     columns(lambda r: 16 + 2 * r, theirs[1, 0], theirs[1, 1])
     columns(lambda r: 17 + 2 * r, theirs[2, 0], theirs[2, 1])
+    for ref in (col_u, col_v, col_i):
+        z_row, x_row = ref[30:31, :], ref[31:32, :]
+        ref[30:31, :] = jnp.concatenate([z_row[:, :64], x_row[:, :64]], axis=1)
+        ref[31:32, :] = jnp.concatenate([z_row[:, 64:], x_row[:, 64:]], axis=1)
 
     def turn(x, carry):
         for n in range(4):
@@ -260,21 +332,37 @@
         def _():
             lax.fori_loop(0, 4, turn, 0)
 
+        @pl.when(i == 2)
+        def _():
+            for k in range(2):
+                for n in range(4):
+                    first_copy(n, k).wait_recv()
+
+        @pl.when(i > 2)
+        def _():
+            for k in range(2):
+                zx_copy(2 * (i - 2), k).wait_recv()
+
         @pl.when(i >= 2)
         def _():
-            for n in range(2):
-                for k in range(2):
-                    zx_copy(2 * (i - 2) + n, k).wait_recv()
-
-        pairs(ROWS + i * 512, 512, coef)
+            for k in range(2):
+                zx_copy(2 * (i - 2) + 1, k).wait_recv()
+
+        first = ROWS + i * 512
+        sweep([(r, first, False, False) for r in range(4)], 512, coef)
         return carry
 
     lax.fori_loop(0, 5, other_step, 0)
 
-    for i in (6, 7):
+    for k in range(2):
+        zx_copy(6, k).wait_recv()
+    first = 4 * ROWS - 2 * CHUNK
+    sweep([(r, first, False, False) for r in range(4)], CHUNK, coef_last)
+    for n in range(2):
         for k in range(2):
-            zx_copy(i, k).wait_recv()
-        pairs(2 * ROWS + i * CHUNK, CHUNK, coef_last, last=i == 7)
+            end_copy(n, k).wait_recv()
+        first = 4 * ROWS - CHUNK + n * 128
+        sweep([(r, first, False, False) for r in range(4)], 128, coef_end, last=n == 1)
 
     line = lax.broadcasted_iota(jnp.int32, (8, 128), 0)
     w_sum = jnp.sum(sums[0], axis=0, keepdims=True)
@@ -282,37 +370,39 @@
     tsend[0] = jnp.where(line == 0, w_sum, jnp.where(line == 1, l_sum, 0.0))
     total_core().start()
 
-    def own_half(x, carry):
-        block = ht[core, x].reshape(CHUNK, ROWS)
-        pown[x] = jnp.dot(block, summed[0], preferred_element_type=jnp.float32)
-        return carry
-
-    lax.fori_loop(0, 4, own_half, 0)
+    own_half(1)
     for i in range(4):
         h_copy(i).wait_recv()
+
+    def mate_part(x, lanes, k):
+        depth = slice(k * 512, (k + 1) * 512)
+        return pown[x, :, lanes] + jnp.dot(
+            htm[x, :, :, :, depth].reshape(CHUNK, 512), summed[1, depth, lanes],
+            preferred_element_type=jnp.float32,
+        )
+
+    for i in range(2):
         p_copy(i).wait_recv()
+    for x in range(4):
+        pown[x] = mate_part(x, slice(0, D), 0)
+    for i in range(2, 4):
+        p_copy(i).wait_recv()
 
     def mate_half(pair):
-        lanes = slice(pair * 256, (pair + 1) * 256)
-
-        def step(x, carry):
-            block = htm[x].reshape(CHUNK, ROWS)
-            v = pown[x, :, lanes] + jnp.dot(
-                block, summed[1, :, lanes], preferred_element_type=jnp.float32
-            )
+        for x in range(4):
+            v = mate_part(x, slice(pair * 256, (pair + 1) * 256), 1)
             v = v.astype(jnp.bfloat16).reshape(4, 4, 16, 256)
             if pair == 0:
-                part1[0, x] = v[..., :128]
+                for y in range(4):
+                    part1[0, :, x, y] = v[y, :, :, :128]
                 part1[1, :, :, x] = v[..., 128:]
             else:
+                part1[2, x] = v[..., :128]
                 for y in range(4):
-                    part1[2, :, x, y] = v[y, :, :, :128]
-                    m = x * (1 - core) + y * core
-                    n = y * (1 - core) + x * core
-                    part1[3, m, :, n] = v[y, :, :, 128:]
-            return carry
-
-        lax.fori_loop(0, 4, step, 0)
+                    for z in range(4):
+                        m = z * (1 - core) + y * core
+                        n = y * (1 - core) + z * core
+                        part1[3, m, x, n] = v[y, z, :, 128:]
         for p in (2 * pair, 2 * pair + 1):
             for ahead in (2, 1, 3):
                 stage_copy(p, 0, ahead).start()
@@ -351,8 +441,12 @@
         core_copy(i).wait_send()
         h_copy(i).wait_send()
         p_copy(i).wait_send()
-    for i in range(8):
-        for k in range(2):
+    for k in range(2):
+        for n in range(4):
+            first_copy(n, k).wait_send()
+        for n in range(2):
+            end_copy(n, k).wait_send()
+        for i in range(1, 7):
             zx_copy(i, k).wait_send()
     total_core().wait_send()
 
@@ -397,13 +491,22 @@
         total_axis(2, ahead).wait_send()
 
 
-def scale_kernel(pair_count, items, gh_ref, gw_ref, tot_ref, gh_out, gw_out, loss_out, buf, sem):
-    scale = 1.0 / math.log(2.0)
+def scale_kernel(
+    pair_count, items, gh_ref, gw_ref, tot_ref, gh_out, gw_out, loss_out, buf, gw_buf, loss_buf, sem
+):
     totals = tot_ref[...]
-    weight_total = totals[0:1, :] * (0.5 * scale)
+    weight_total = totals[0:1, :] * (0.5 / math.log(2.0))
     pair_loss = totals[1:2, :] * 0.5
     inverse = float(pair_count) / weight_total
-    across = jnp.broadcast_to(jnp.concatenate([inverse] * 16, axis=1), (8, FF))
+    across = jnp.broadcast_to(jnp.concatenate([inverse] * 16, axis=1), (16, FF))
+    gw_buf[...] = gw_ref[...] * (across[:, :D] * (1.0 / items))
+    loss_buf[...] = (pair_loss / weight_total)[:, 0:1]
+    small = (
+        pltpu.make_async_copy(gw_buf, gw_out, sem.at[8]),
+        pltpu.make_async_copy(loss_buf, loss_out, sem.at[9]),
+    )
+    for copy in small:
+        copy.start()
 
     def out(i):
         rows = pl.ds(i * 128, 128)
@@ -412,13 +515,12 @@
     for i in range(8):
         for n in range(8):
             rows = slice(i * 128 + n * 16, i * 128 + (n + 1) * 16)
-            v = gh_ref[rows, :].astype(jnp.float32) * jnp.concatenate([across] * 2, axis=0)
-            buf[rows, :] = v.astype(jnp.bfloat16)
+            buf[rows, :] = (gh_ref[rows, :].astype(jnp.float32) * across).astype(jnp.bfloat16)
         out(i).start()
-    gw_out[...] = gw_ref[...] * (across[0:1, :D] * (1.0 / items))
-    loss_out[...] = (pair_loss / weight_total)[:, 0:1]
     for i in range(8):
         out(i).wait()
+    for copy in small:
+        copy.wait()
 
 
 def on_device(hidden, weight, stamps, group_ids):
@@ -444,13 +546,13 @@
             vm((2, 8, 128), jnp.int32), vm((3, 2, 8, 128), jnp.int32),
             vm((32, 128), f32), vm((32, 128), f32), vm((32, 128), f32),
             vm((ROWS, 128), f32), vm((ROWS, 128), f32), vm((ROWS, 128), f32),
-            vm((ROWS, D), f32), vm((2, ROWS, D), bf), vm((ROWS, 512), bf), vm((ROWS, CHUNK), bf),
+            vm((ROWS, D), f32), vm((2, ROWS, D), bf), vm((ROWS, 512), bf), vm((ROWS, CHUNK), bf), vm((ROWS, 128), bf),
             vm((2, 8, 128), f32), vm((4, CHUNK, D), f32),
             vm((4, 4, 4, 4, 16, 128), bf), vm((4, 4, 4, 16, 128), bf), vm((4, 4, 16, 128), bf),
             vm((4, 3, 4, 4, 16, 128), bf), vm((4, 3, 4, 16, 128), bf), vm((4, 3, 16, 128), bf),
             vm((4, 8, 128), f32), vm((8, 128), f32), vm((3, 4, 8, 128), f32),
-            sem((11,)), sem((3,)), sem((3,)), sem((4,)), sem((4,)),
-            sem((2, 8)), sem((2, 8)), sem((4,)), sem((4,)), sem((4,)), sem((4,)),
+            sem((15,)), sem((3,)), sem((3,)), sem((4,)), sem((4,)),
+            sem((2, 8)), sem((2, 8)), sem((2, 4)), sem((2, 4)), sem((2, 2)), sem((2, 2)), sem((4,)), sem((4,)), sem((4,)), sem((4,)),
             sem((4, 3)), sem((4, 3)), sem((4, 3)), sem((4, 3)), sem((4, 3)), sem((4, 3)),
             sem, sem, sem((3, 3)), sem((3, 3)),
         ],
@@ -474,8 +576,8 @@
             jax.ShapeDtypeStruct((1, 1), f32),
         ),
         in_specs=[local, local, local],
-        out_specs=(whole, local, local),
-        scratch_shapes=[vm((ROWS, FF), bf), sem((8,))],
+        out_specs=(whole, whole, whole),
+        scratch_shapes=[vm((ROWS, FF), bf), vm((16, D), f32), vm((1, 1), f32), sem((10,))],
         compiler_params=pltpu.CompilerParams(vmem_limit_bytes=16 << 20),
         cost_estimate=pl.CostEstimate(
             flops=2 << 20, bytes_accessed=4 << 20, transcendentals=0

time: 55.6 us -> 54.8 us (0.986)
  Pallas kernels: 54.8 us -> 54 us
    pallas_call x1, Pallas kernels: 2.78 us -> 2.19 us  [on_device(): pl.pallas_call(functools.partial(scale_kernel, pair_count, items), out_sh...]
where the time goes in v3:
time: 54.8 us; the launch traced here: 54.6 us
  Pallas kernels  54 us (99%)
  between operations  0.64 us (1%)
    pallas_call x1, Pallas kernels, on_device(): pl.pallas_call(kernel, out_shape=(pltpu.VMEM((ROWS, FF), bf), pltpu.VMEM(...  51.8 us
    pallas_call x1, Pallas kernels, on_device(): pl.pallas_call(functools.partial(scale_kernel, pair_count, items), out_sh...  2.19 us

profile of v3, /device:TPU:0, one launch (start us, length us, event | category | flops | bytes accessed | tf_op | source)
XLA Modules:
  0.0 54.6 jit_solution(16455686297522625642)
XLA Ops:
  0.6 51.8 %shard_map.67 = (bf16[1024,2048]{1,0:T(8,128)(2,1)S(1)}, f32[16,512]{1,0:T(8,128)S(1)}, f32[8,128]{1,0:T(8,128)S(1)}) custom-call(bf16[1024,2048]{1,0:T(8,128)(2,1)} %hidden_hbm.1, bf16[2048,512]{1,0:T(8,128)(2,1)} %weight_hbm.1, s32[8,128]{1,0:T(8,128)} %bitcast.3, s32[8,128]{1,0:T(8,128)} %bitcast.4), custom_call_target="tpu_custom_call" | custom-call | flops 15000000512 | bytes 7340032 | tf_op jit(solution)/shard_map/pallas_call | solution.py:534
  52.5 2.2 %shard_map.68 = (bf16[1024,2048]{1,0:T(8,128)(2,1)}, f32[16,512]{1,0:T(8,128)}, f32[1,1]{1,0:T(1,128)}) custom-call(bf16[1024,2048]{1,0:T(8,128)(2,1)S(1)} %get-tuple-element.9.gh_ref, f32[16,512]{1,0:T(8,128)S(1)} %get-tuple-element.10.gw_ref, f32[8,128]{1,0:T(8,128)S(1)} %get-tuple-element.11.tot_ref), custom_call_target="tpu_custom_call" | custom-call | flops 2097152 | bytes 4194304 | tf_op jit(solution)/shard_map/pallas_call | solution.py:571

commit v4 on v3

--- a/solution.py
+++ b/solution.py
@@ -16,6 +16,7 @@
 MESH = pl.DeviceIdType.MESH
 NT = (((1,), (1,)), ((), ()))
 TN = (((0,), (0,)), ((), ()))
+SMALL = 2.0**-12
 SCALE2 = math.log2(math.e) / math.sqrt(D)
 ORDERS = ("zxy", "yzx", "xyz", "mxn")
 
@@ -270,7 +271,9 @@
                     cu, cv, ci = cols[h]
                     sign = jnp.where(ri == ci, -SCALE2, SCALE2)
                     m = s[q * 32 : (q + 1) * 32, h * 128 : (h + 1) * 128] * sign
-                    plus = jnp.maximum(m, jnp.log2(1.0 + jnp.exp2(jnp.minimum(m, 100.0))))
+                    e = jnp.exp2(jnp.minimum(m, 100.0))
+                    near = jnp.where(e < SMALL, e * math.log2(math.e), jnp.log2(1.0 + e))
+                    plus = jnp.maximum(m, near)
                     w = jnp.minimum(ru * cv, rv * cu)
                     if diagonal and lo // 128 == first // 128 + h:
                         i = lax.broadcasted_iota(jnp.int32, (32, 128), 0) + lo % 128

time: 54.8 us -> 54.9 us (level)
  no operation moved by 1% of the time
where the time goes in v4:
time: 54.9 us; the launch traced here: 54.8 us
  Pallas kernels  54.2 us (99%)
  between operations  0.64 us (1%)
    pallas_call x1, Pallas kernels, on_device(): pl.pallas_call(kernel, out_shape=(pltpu.VMEM((ROWS, FF), bf), pltpu.VMEM(...  52 us
    pallas_call x1, Pallas kernels, on_device(): pl.pallas_call(functools.partial(scale_kernel, pair_count, items), out_sh...  2.19 us

profile of v4, /device:TPU:0, one launch (start us, length us, event | category | flops | bytes accessed | tf_op | source)
XLA Modules:
  0.0 54.8 jit_solution(14458144171827906635)
XLA Ops:
  0.6 52.0 %shard_map.67 = (bf16[1024,2048]{1,0:T(8,128)(2,1)S(1)}, f32[16,512]{1,0:T(8,128)S(1)}, f32[8,128]{1,0:T(8,128)S(1)}) custom-call(bf16[1024,2048]{1,0:T(8,128)(2,1)} %hidden_hbm.1, bf16[2048,512]{1,0:T(8,128)(2,1)} %weight_hbm.1, s32[8,128]{1,0:T(8,128)} %bitcast.3, s32[8,128]{1,0:T(8,128)} %bitcast.4), custom_call_target="tpu_custom_call" | custom-call | flops 15000000512 | bytes 7340032 | tf_op jit(solution)/shard_map/pallas_call | solution.py:537
  52.6 2.2 %shard_map.68 = (bf16[1024,2048]{1,0:T(8,128)(2,1)}, f32[16,512]{1,0:T(8,128)}, f32[1,1]{1,0:T(1,128)}) custom-call(bf16[1024,2048]{1,0:T(8,128)(2,1)S(1)} %get-tuple-element.9.gh_ref, f32[16,512]{1,0:T(8,128)S(1)} %get-tuple-element.10.gw_ref, f32[8,128]{1,0:T(8,128)S(1)} %get-tuple-element.11.tot_ref), custom_call_target="tpu_custom_call" | custom-call | flops 2097152 | bytes 4194304 | tf_op jit(solution)/shard_map/pallas_call | solution.py:574
